TPU v7x, 32 devices: a whole 2x2x4 slice. The times are simulated.
32 devices in a mesh: ctx: 4 (over x, core), row: 4 (over z), col: 2 (over y).
Axes of the slice: x: 2, y: 2, z: 4, core: 2. Of those that a mesh axis runs over, the one named last changes fastest.
Arguments:
- states: bfloat16 [384, 4096], P('ctx', 'row'), may hold values from -6 to 6
- context: bfloat16 [384, 4096], P('ctx', 'row'), may hold values from -6 to 6
- up_weight: bfloat16 [4096, 8192], P('row', 'col'), may hold values from -0.09375 to 0.09375
- down_weight: bfloat16 [8192, 4096], P('col', 'row'), may hold values from -0.0625 to 0.0625
- cotangent: bfloat16 [384, 4096], P('ctx', 'row'), may hold values from -6 to 6
Outputs:
- latent: bfloat16 [384, 4096], P('ctx', 'row')
- logdet: float32 [384], P(('ctx', 'row'))
- grad_states: bfloat16 [384, 4096], P('ctx', 'row')
- grad_context: bfloat16 [384, 4096], P('ctx', 'row')
- grad_up: float32 [4096, 8192], P('row', 'col')
- grad_down: float32 [8192, 4096], P('col', 'row')
All inputs are finite; a program needn't handle non-finite values.
Results may differ from a plain program's by a relative error of at most 0.024.
Values may be sent and summed in bfloat16 or wider, within the bound.
A program may use at most 192 MiB of HBM per device.

v0:
```python
import jax
import jax.numpy as jnp
from jax import lax
from jax.sharding import PartitionSpec as P


def silu_slope(hidden):
    sigmoid_part = jax.nn.sigmoid(hidden)
    return sigmoid_part * (1.0 + hidden * (1.0 - sigmoid_part))


def collect(row_block):
    return lax.all_gather(row_block, "row", axis=0, tiled=True)


def feature_total(partial_terms):
    return lax.psum(partial_terms.astype(jnp.bfloat16), "col").astype(jnp.float32)


def contract(left_side, right_side, left_dim, right_dim):
    return lax.dot_general(
        left_side,
        right_side,
        (((left_dim,), (right_dim,)), ((), ())),
        preferred_element_type=jnp.float32,
    )


def shards(states, context, up_weight, down_weight, cotangent):
    hidden = lax.psum_scatter(
        jnp.dot(context, up_weight, preferred_element_type=jnp.float32).astype(jnp.bfloat16),
        "row",
        scatter_dimension=0,
        tiled=True,
    ).astype(jnp.float32)
    activations = collect(jax.nn.silu(hidden).astype(jnp.bfloat16))
    output_terms = jnp.dot(activations, down_weight, preferred_element_type=jnp.float32)
    mixed_total = feature_total(output_terms)
    log_scale = jnp.tanh(mixed_total)
    shrink = jnp.exp(-log_scale)
    flowed = states.astype(jnp.float32) * shrink
    cotangent_wide = cotangent.astype(jnp.float32)
    det_terms = -jnp.sum(log_scale, axis=1)
    scale_rows = ((1.0 - cotangent_wide * flowed) * (1.0 - log_scale * log_scale)).astype(
        jnp.bfloat16
    )
    down_part = contract(activations, scale_rows, 0, 0)
    grad_down = lax.psum(down_part.astype(jnp.bfloat16), "ctx").astype(jnp.float32)
    back_terms = contract(scale_rows, down_weight, 1, 1)
    back_rows = lax.psum_scatter(
        back_terms.astype(jnp.bfloat16), "row", scatter_dimension=0, tiled=True
    ).astype(jnp.float32)
    logdet = lax.psum_scatter(det_terms, "row", scatter_dimension=0, tiled=True)
    slope_rows = (back_rows * silu_slope(hidden)).astype(jnp.bfloat16)
    slope_all = collect(slope_rows)
    input_terms = contract(slope_all, up_weight, 1, 1)
    grad_states = (cotangent_wide * shrink).astype(jnp.bfloat16)
    grad_context = feature_total(input_terms).astype(jnp.bfloat16)
    up_part = contract(context, slope_all, 0, 0)
    grad_up = lax.psum(up_part.astype(jnp.bfloat16), "ctx").astype(jnp.float32)
    return (flowed.astype(jnp.bfloat16), logdet, grad_states, grad_context, grad_up, grad_down)


def solution(mesh):
    placed = (P("ctx", "row"), P("ctx", "row"), P("row", "col"), P("col", "row"), P("ctx", "row"))
    return jax.shard_map(
        shards,
        mesh=mesh,
        in_specs=placed,
        out_specs=(
            P("ctx", "row"),
            P(("ctx", "row")),
            P("ctx", "row"),
            P("ctx", "row"),
            P("row", "col"),
            P("col", "row"),
        ),
        check_vma=False,
    )
```

profile of v0, /device:TPU:0, one launch (start us, length us, event | category | flops | bytes accessed | tf_op | source)
XLA Modules:
  0.0 463.3 jit_solution(15541179772895529971)
XLA Ops:
  7.2 0.0 copy-start
  7.2 0.0 reduce-scatter.3.cloned.1.call-start
  7.2 0.9 copy-done
  8.1 5.7 %convolution_convert_fusion.2 = bf16[96,4096]{1,0:T(8,128)(2,1)} fusion(bf16[96,1024]{1,0:T(8,128)(2,1)S(1)} %copy-done, bf16[1024,4096]{1,0:T(8,128)(2,1)} %param.7), kind=kOutput, calls=%fused_computation.3 | convolution fusion | flops 805699584 | bytes 9371648 | tf_op jit(solution)/shard_map/dot_general | solution.py:31
  13.8 0.0 reduce-scatter.3.cloned.1.call-update
  13.8 0.0 all-reduce.6.cloned.1.call-start
  13.9 26.1 %reduce-scatter.3.cloned.1.call-done = bf16[24,4096]{1,0:T(8,128)(2,1)} async-done(((bf16[96,4096]{1,0:T(8,128)(2,1)}), bf16[24,4096]{1,0:T(8,128)(2,1)}) %reduce-scatter.3.cloned.1.call-update) | async-done | bytes 196624 | tf_op jit(solution)/shard_map/reduce_scatter | solution.py:30
  40.0 1.0 fusion.7
  41.0 18.0 %all_gather.6 = bf16[96,4096]{1,0:T(8,128)(2,1)S(1)} all-gather(bf16[24,4096]{1,0:T(8,128)(2,1)S(1)} %fusion.7), channel_id=1, replica_groups=mesh['ctx'=4,'row'=4,'col'=2] {'row'}, dimensions={0}, use_global_device_ids=true | all-gather | bytes 983040 | tf_op jit(solution)/shard_map/all_gather | solution.py:13
  59.0 0.0 copy-start.2
  59.0 0.0 copy-start.3
  59.0 5.6 %convolution_convert_fusion.4 = bf16[96,1024]{1,0:T(8,128)(2,1)} fusion(bf16[96,4096]{1,0:T(8,128)(2,1)S(1)} %all_gather.6, bf16[4096,1024]{1,0:T(8,128)(2,1)} %param.8), kind=kOutput, calls=%fused_computation.5 | convolution fusion | flops 805404672 | bytes 9371648 | tf_op jit(solution)/shard_map/dot_general | solution.py:37
  64.6 0.0 all-reduce.6.cloned.1.call-update
  64.6 0.0 reduce-scatter.5.cloned.1.call-start
  64.7 21.7 %all-reduce.6.cloned.1.call-done = bf16[96,1024]{1,0:T(8,128)(2,1)} async-done(((bf16[96,1024]{1,0:T(8,128)(2,1)}), bf16[96,1024]{1,0:T(8,128)(2,1)}) %all-reduce.6.cloned.1.call-update) | async-done | bytes 196624 | tf_op jit(solution)/shard_map/psum | solution.py:17
  86.4 0.0 copy-done.2
  86.4 0.0 copy-done.3
  86.4 0.0 copy-start.4
  86.4 7.1 %convolution_convert_fusion.1 = bf16[96,4096]{1,0:T(8,128)(2,1)} fusion(bf16[4096,1024]{1,0:T(8,128)(2,1)} %param.8, bf16[96,1024]{1,0:T(8,128)(2,1)S(1)} %copy-done.2, bf16[96,1024]{1,0:T(8,128)(2,1)} %all-reduce.6.cloned.1.call-done, bf16[96,1024]{1,0:T(8,128)(2,1)S(1)} %copy-done.3), kind=kOutput, calls=%fused_computation.2 | convolution fusion | flops 806780928 | bytes 9764864 | tf_op jit(solution)/shard_map/dot_general | solution.py:21
  93.5 0.0 copy-start.5
  93.5 0.0 reduce-scatter.5.cloned.1.call-update
  93.5 0.0 all-reduce.10.cloned.1.call-start
  93.6 0.0 copy-done.4
  93.6 5.8 %convolution_convert_fusion = bf16[4096,1024]{1,0:T(8,128)(2,1)} fusion(bf16[96,4096]{1,0:T(8,128)(2,1)S(1)} %all_gather.6, bf16[96,1024]{1,0:T(8,128)(2,1)S(1)} %copy-done.2, bf16[96,1024]{1,0:T(8,128)(2,1)S(1)} %copy-done.4, bf16[96,1024]{1,0:T(8,128)(2,1)S(1)} %copy-done.3), kind=kOutput, calls=%fused_computation.1 | convolution fusion | flops 810582016 | bytes 9764864 | tf_op jit(solution)/shard_map/dot_general | solution.py:21
  99.4 17.6 %reduce-scatter.5.cloned.1.call-done = bf16[24,4096]{1,0:T(8,128)(2,1)} async-done(((bf16[96,4096]{1,0:T(8,128)(2,1)}), bf16[24,4096]{1,0:T(8,128)(2,1)}) %reduce-scatter.5.cloned.1.call-update) | async-done | bytes 196624 | tf_op jit(solution)/shard_map/reduce_scatter | solution.py:50
  117.0 0.0 copy-done.5
  117.0 1.1 fusion.11
  118.1 17.9 %all_gather.7 = bf16[96,4096]{1,0:T(8,128)(2,1)S(1)} all-gather(bf16[24,4096]{1,0:T(8,128)(2,1)S(1)} %fusion.11), channel_id=1, replica_groups=mesh['ctx'=4,'row'=4,'col'=2] {'row'}, dimensions={0}, use_global_device_ids=true | all-gather | bytes 983040 | tf_op jit(solution)/shard_map/all_gather | solution.py:13
  136.1 5.8 %convert_bitcast_fusion = bf16[1024,4096]{0,1:T(8,128)(2,1)} fusion(bf16[96,4096]{1,0:T(8,128)(2,1)S(1)} %all_gather.7, bf16[96,1024]{1,0:T(8,128)(2,1)S(1)} %copy-done), kind=kOutput, calls=%fused_computation | convolution fusion | flops 809500672 | bytes 9371648 | tf_op jit(solution)/shard_map/dot_general | solution.py:21
  141.8 0.0 copy-start.6
  141.8 0.0 all-reduce.10.cloned.1.call-update
  141.9 0.2 all-reduce.8.cloned.1.call-start
  142.1 0.4 copy-done.6
  142.5 0.6 dynamic-slice
  143.7 7.2 %convolution_convert_fusion.3 = bf16[96,1024]{1,0:T(8,128)(2,1)} fusion(bf16[96,4096]{1,0:T(8,128)(2,1)S(1)} %all_gather.7, bf16[1024,4096]{1,0:T(8,128)(2,1)} %param.7), kind=kOutput, calls=%fused_computation.4 | convolution fusion | flops 805404672 | bytes 9371648 | tf_op jit(solution)/shard_map/dot_general | solution.py:21
  150.9 0.0 all-reduce.8.cloned.1.call-update
  151.0 1.0 fusion
  152.0 9.6 %all-reduce = f32[96]{0:T(128)S(1)} all-reduce(f32[96]{0:T(128)S(1)} %neg.13), channel_id=3, replica_groups=mesh['ctx'=4,'row'=4,'col'=2] {'row'}, use_global_device_ids=true, to_apply=%region_3.4.clone | all-reduce | flops 96 | bytes 768
  161.6 0.6 dynamic-slice.1
  162.2 268.0 %all-reduce.10.cloned.1.call-done = (bf16[1024,4096]{0,1:T(8,128)(2,1)}, bf16[4096,1024]{1,0:T(8,128)(2,1)}) async-done(((bf16[1024,4096]{0,1:T(8,128)(2,1)}, bf16[4096,1024]{1,0:T(8,128)(2,1)}), (bf16[1024,4096]{0,1:T(8,128)(2,1)}, bf16[4096,1024]{1,0:T(8,128)(2,1)})) %all-reduce.10.cloned.1.call-update) | async-done | bytes 16777232 | tf_op jit(solution)/shard_map/psum | solution.py:60
  430.1 12.3 %copy.12 = f32[1024,4096]{1,0:T(8,128)} copy(bf16[1024,4096]{0,1:T(8,128)(2,1)} %get-tuple-element.18) | data formatting | bytes 25165824
  442.5 0.0 copy-start.1
  442.5 11.8 %convert_element_type.77 = f32[4096,1024]{1,0:T(8,128)} convert(bf16[4096,1024]{1,0:T(8,128)(2,1)} %get-tuple-element.19) | non-fusion elementwise | flops 4194304 | bytes 25165824 | tf_op jit(solution)/shard_map/convert_element_type | solution.py:48
  454.2 1.0 all-reduce.8.cloned.1.call-done
  455.2 1.6 copy.17
  456.8 0.0 copy-done.1
  (1 shorter events, 0.0 us)
Async XLA Ops:
  7.2 0.9 copy-start
  7.2 32.8 %reduce-scatter.3.cloned.1.call-start = ((), (), s32[]{:S(2)}) async-start(), calls=%async_computation.2 | async-start | bytes 983040 | tf_op jit(solution)/shard_map/reduce_scatter | solution.py:30
  13.8 72.5 %all-reduce.6.cloned.1.call-start = ((), (), s32[]{:S(2)}) async-start(), calls=%async_computation.3 | async-start | bytes 393216 | tf_op jit(solution)/shard_map/psum | solution.py:17
  59.0 27.3 %copy-start.2 = (bf16[96,1024]{1,0:T(8,128)(2,1)S(1)}, bf16[96,1024]{1,0:T(8,128)(2,1)}, u32[]{:S(2)}) copy-start(bf16[96,1024]{1,0:T(8,128)(2,1)} %param.9) | copy-start | bytes 589828
  59.0 27.3 %copy-start.3 = (bf16[96,1024]{1,0:T(8,128)(2,1)S(1)}, bf16[96,1024]{1,0:T(8,128)(2,1)}, u32[]{:S(2)}) copy-start(bf16[96,1024]{1,0:T(8,128)(2,1)} %param.5) | copy-start | bytes 589828
  64.6 52.4 %reduce-scatter.5.cloned.1.call-start = ((), (), s32[]{:S(2)}) async-start(), calls=%async_computation.4 | async-start | bytes 983040 | tf_op jit(solution)/shard_map/reduce_scatter | solution.py:50
  86.4 7.2 %copy-start.4 = (bf16[96,1024]{1,0:T(8,128)(2,1)S(1)}, bf16[96,1024]{1,0:T(8,128)(2,1)}, u32[]{:S(2)}) copy-start(bf16[96,1024]{1,0:T(8,128)(2,1)} %all-reduce.6.cloned.1.call-done) | copy-start | bytes 589828
  93.5 23.5 %copy-start.5 = (bf16[24,4096]{1,0:T(8,128)(2,1)S(1)}, bf16[24,4096]{1,0:T(8,128)(2,1)}, u32[]{:S(2)}) copy-start(bf16[24,4096]{1,0:T(8,128)(2,1)} %reduce-scatter.3.cloned.1.call-done) | copy-start | bytes 589828
  93.5 336.6 %all-reduce.10.cloned.1.call-start = ((), (), s32[]{:S(2)}) async-start(), calls=%async_computation.6 | async-start | bytes 33554432 | tf_op jit(solution)/shard_map/psum | solution.py:60
  141.8 0.7 copy-start.6
  141.9 313.3 %all-reduce.8.cloned.1.call-start = ((), (), s32[]{:S(2)}) async-start(), calls=%async_computation.5 | async-start | bytes 393216 | tf_op jit(solution)/shard_map/psum | solution.py:17
  442.5 14.3 %copy-start.1 = (bf16[96,1024]{1,0:T(8,128)(2,1)S(1)}, bf16[96,1024]{1,0:T(8,128)(2,1)}, u32[]{:S(2)}) copy-start(bf16[96,1024]{1,0:T(8,128)(2,1)} %param.6) | copy-start | bytes 589828
Sparse Core Ops, SparseCore 0:
  14.0 25.9 reduce-scatter.2
  64.7 21.5 all-reduce.5
  93.6 23.3 reduce-scatter.4
  142.0 288.0 all-reduce.9
  432.8 22.3 all-reduce.7
where the time goes:
time: 464 us; the launch traced here: 463 us
  waiting for transfers between devices  334 us (72%)
  blocking collectives  45.5 us (10%)
  matrix products  37.2 us (8%)
  local copies, waits for them, and re-layouts  16.4 us (4%)
  other arithmetic  14.9 us (3%)
  between operations  14.5 us (3%)
    psum x1, waiting for transfers between devices, shards(): grad_up = lax.psum(up_part.astype(jnp.bfloat16), 'ctx').astype(jnp.float32)  268 us
    all_gather x2, blocking collectives, collect(): return lax.all_gather(row_block, 'row', axis=0, tiled=True)  35.9 us
    reduce_scatter x1, waiting for transfers between devices, shards(): lax.psum_scatter(jnp.dot(context, up_weight, preferred_element_type=jnp.f...  26.1 us
    dot_general x4, matrix products, contract(): lax.dot_general(left_side, right_side, (((left_dim,), (right_dim,)), ((),...  25.9 us
    psum x2, waiting for transfers between devices, feature_total(): lax.psum(partial_terms.astype(jnp.bfloat16), 'col').astype(jnp.float32)  22.6 us
    reduce_scatter x1, waiting for transfers between devices, shards(): lax.psum_scatter(back_terms.astype(jnp.bfloat16), 'row', scatter_dimensio...  17.6 us
    unnamed x18, local copies, waits for them, and re-layouts  16.4 us
    convert_element_type x1, other arithmetic, shards(): lax.psum(down_part.astype(jnp.bfloat16), 'ctx').astype(jnp.float32)  11.8 us
  transfers between devices with their start and end apart: 5, of which 5 were waited for; matrix products, arithmetic and copies ran while one was open for 8% of the time, Pallas kernels for 0%

commit v1 on v0

--- a/solution.py
+++ b/solution.py
@@ -2,6 +2,19 @@
 import jax.numpy as jnp
 from jax import lax
 from jax.sharding import PartitionSpec as P
+
+
+def ring_gather(array, axis, dim):
+    ways = lax.axis_size(axis)
+    up = [(d, (d + 1) % ways) for d in range(ways)]
+    down = [(d, (d - 1) % ways) for d in range(ways)]
+    earlier, later = ([array], [array])
+    for _ in range(ways // 2):
+        earlier.append(lax.ppermute(earlier[-1], axis, up))
+    for _ in range((ways - 1) // 2):
+        later.append(lax.ppermute(later[-1], axis, down))
+    line = jnp.concatenate([*earlier[::-1], *later[1:]], axis=dim)
+    return jnp.roll(line, (lax.axis_index(axis) - ways // 2) * array.shape[dim], axis=dim)
 
 
 def silu_slope(hidden):
@@ -10,7 +23,7 @@
 
 
 def collect(row_block):
-    return lax.all_gather(row_block, "row", axis=0, tiled=True)
+    return ring_gather(row_block, "row", 0)
 
 
 def feature_total(partial_terms):

time: 464 us -> 466 us (level)
  blocking collectives: 45.5 us -> 10.5 us
  waiting for transfers between devices: 334 us -> 359 us
  starting transfers between devices: 0.39 us -> 7.95 us
  other arithmetic: 14.9 us -> 19.9 us
    all_gather x2 -> x0, blocking collectives: 35.9 us -> none  [collect(): return lax.all_gather(row_block, 'row', axis=0, tiled=True)]
    ppermute x0 -> x6, waiting for transfers between devices: none -> 20.2 us  [the longest x4 19.3 us: ring_gather(): earlier.append(lax.ppermute(earlier[-1], axis, up))]
    ppermute x0 -> x6, starting transfers between devices: none -> 7.74 us  [the longest x2 7.62 us: ring_gather(): later.append(lax.ppermute(later[-1], axis, down))]
    reduce_scatter x1, waiting for transfers between devices: 17.6 us -> 23.4 us  [shards(): lax.psum_scatter(back_terms.astype(jnp.bfloat16), 'row', scatter_dimensio...]
    concatenate x0 -> x2, other arithmetic: none -> 5 us  [ring_gather(): jnp.roll(line, (lax.axis_index(axis) - ways // 2) * array.shape[dim], axi...]
  transfers between devices with their start and end apart: 5 -> 11, of which waited for: 5 -> 10; matrix products, arithmetic and copies ran while one was open for 8% -> 8% of each run, Pallas kernels for 0% -> 0%
where the time goes in v1:
time: 466 us; the launch traced here: 465 us
  waiting for transfers between devices  359 us (77%)
  matrix products  36.8 us (8%)
  other arithmetic  19.9 us (4%)
  local copies, waits for them, and re-layouts  16.6 us (4%)
  between operations  14.5 us (3%)
  blocking collectives  10.5 us (2%)
  starting transfers between devices  7.95 us (2%)
    psum x1, waiting for transfers between devices, shards(): grad_up = lax.psum(up_part.astype(jnp.bfloat16), 'ctx').astype(jnp.float32)  268 us
    reduce_scatter x1, waiting for transfers between devices, shards(): lax.psum_scatter(jnp.dot(context, up_weight, preferred_element_type=jnp.f...  26.1 us
    dot_general x4, matrix products, contract(): lax.dot_general(left_side, right_side, (((left_dim,), (right_dim,)), ((),...  25.5 us
    reduce_scatter x1, waiting for transfers between devices, shards(): lax.psum_scatter(back_terms.astype(jnp.bfloat16), 'row', scatter_dimensio...  23.4 us
    psum x2, waiting for transfers between devices, feature_total(): lax.psum(partial_terms.astype(jnp.bfloat16), 'col').astype(jnp.float32)  21.5 us
    ppermute x4, waiting for transfers between devices, ring_gather(): earlier.append(lax.ppermute(earlier[-1], axis, up))  19.3 us
    unnamed x18, local copies, waits for them, and re-layouts  16.6 us
    convert_element_type x1, other arithmetic, shards(): lax.psum(down_part.astype(jnp.bfloat16), 'ctx').astype(jnp.float32)  11.8 us
  transfers between devices with their start and end apart: 11, of which 10 were waited for; matrix products, arithmetic and copies ran while one was open for 8% of the time, Pallas kernels for 0%

profile of v1, /device:TPU:0, one launch (start us, length us, event | category | flops | bytes accessed | tf_op | source)
XLA Modules:
  0.0 465.5 jit_solution(10602310360964570282)
XLA Ops:
  7.2 0.0 copy-start
  7.2 0.0 reduce-scatter.3.cloned.1.call-start
  7.2 0.9 copy-done
  8.1 5.7 %convolution_convert_fusion.2 = bf16[96,4096]{1,0:T(8,128)(2,1)} fusion(bf16[96,1024]{1,0:T(8,128)(2,1)S(1)} %copy-done, bf16[1024,4096]{1,0:T(8,128)(2,1)} %param.9), kind=kOutput, calls=%fused_computation.3 | convolution fusion | flops 805699584 | bytes 9371648 | tf_op jit(solution)/shard_map/dot_general | solution.py:44
  13.8 0.0 reduce-scatter.3.cloned.1.call-update
  13.8 0.0 all-reduce.6.cloned.1.call-start
  13.9 26.1 %reduce-scatter.3.cloned.1.call-done = bf16[24,4096]{1,0:T(8,128)(2,1)} async-done(((bf16[96,4096]{1,0:T(8,128)(2,1)}), bf16[24,4096]{1,0:T(8,128)(2,1)}) %reduce-scatter.3.cloned.1.call-update) | async-done | bytes 196624 | tf_op jit(solution)/shard_map/reduce_scatter | solution.py:43
  40.0 1.0 fusion.21
  41.0 0.1 collective-permute-start
  41.1 3.8 collective-permute-start.2
  44.9 5.5 %collective-permute-done = bf16[24,4096]{1,0:T(8,128)(2,1)S(1)} collective-permute-done((bf16[24,4096]{1,0:T(8,128)(2,1)S(1)}, bf16[24,4096]{1,0:T(8,128)(2,1)S(1)}, u32[]{:S(2)}, u32[]{:S(2)}) %collective-permute-start) | collective-permute-done | bytes 196640 | tf_op jit(solution)/shard_map/ppermute | solution.py:13
  50.4 0.0 collective-permute-start.1
  50.4 0.9 collective-permute-done.2
  51.3 6.6 %collective-permute-done.1 = bf16[24,4096]{1,0:T(8,128)(2,1)S(1)} collective-permute-done((bf16[24,4096]{1,0:T(8,128)(2,1)S(1)}, bf16[24,4096]{1,0:T(8,128)(2,1)S(1)}, u32[]{:S(2)}, u32[]{:S(2)}) %collective-permute-start.1) | collective-permute-done | bytes 196640 | tf_op jit(solution)/shard_map/ppermute | solution.py:13
  57.9 2.5 fusion.10
  60.4 0.0 copy-start.2
  60.4 0.0 copy-start.3
  60.4 5.6 %convolution_convert_fusion.4 = bf16[96,1024]{1,0:T(8,128)(2,1)} fusion(bf16[96,4096]{1,0:T(8,128)(2,1)S(1)} %fusion.10, bf16[4096,1024]{1,0:T(8,128)(2,1)} %param.10), kind=kOutput, calls=%fused_computation.21 | convolution fusion | flops 805404672 | bytes 9371648 | tf_op jit(solution)/shard_map/dot_general | solution.py:50
  66.0 0.0 all-reduce.6.cloned.1.call-update
  66.0 0.0 copy-start.5
  66.0 0.0 reduce-scatter.5.cloned.1.call-start
  66.1 20.6 %all-reduce.6.cloned.1.call-done = bf16[96,1024]{1,0:T(8,128)(2,1)} async-done(((bf16[96,1024]{1,0:T(8,128)(2,1)}), bf16[96,1024]{1,0:T(8,128)(2,1)}) %all-reduce.6.cloned.1.call-update) | async-done | bytes 196624 | tf_op jit(solution)/shard_map/psum | solution.py:30
  86.7 0.0 copy-done.2
  86.7 0.0 copy-done.3
  86.7 0.0 copy-start.4
  86.7 7.1 %convolution_convert_fusion.1 = bf16[96,4096]{1,0:T(8,128)(2,1)} fusion(bf16[4096,1024]{1,0:T(8,128)(2,1)} %param.10, bf16[96,1024]{1,0:T(8,128)(2,1)S(1)} %copy-done.2, bf16[96,1024]{1,0:T(8,128)(2,1)} %all-reduce.6.cloned.1.call-done, bf16[96,1024]{1,0:T(8,128)(2,1)S(1)} %copy-done.3), kind=kOutput, calls=%fused_computation.2 | convolution fusion | flops 806780928 | bytes 9764864 | tf_op jit(solution)/shard_map/dot_general | solution.py:34
  93.8 0.0 reduce-scatter.5.cloned.1.call-update
  93.8 0.0 all-reduce.10.cloned.1.call-start
  93.9 23.4 %reduce-scatter.5.cloned.1.call-done = bf16[24,4096]{1,0:T(8,128)(2,1)} async-done(((bf16[96,4096]{1,0:T(8,128)(2,1)}), bf16[24,4096]{1,0:T(8,128)(2,1)}) %reduce-scatter.5.cloned.1.call-update) | async-done | bytes 196624 | tf_op jit(solution)/shard_map/reduce_scatter | solution.py:63
  117.3 0.0 copy-done.5
  117.3 1.1 fusion.25
  118.4 0.1 collective-permute-start.3
  118.4 3.8 collective-permute-start.5
  122.2 5.5 %collective-permute-done.3 = bf16[24,4096]{1,0:T(8,128)(2,1)S(1)} collective-permute-done((bf16[24,4096]{1,0:T(8,128)(2,1)S(1)}, bf16[24,4096]{1,0:T(8,128)(2,1)S(1)}, u32[]{:S(2)}, u32[]{:S(2)}) %collective-permute-start.3) | collective-permute-done | bytes 196640 | tf_op jit(solution)/shard_map/ppermute | solution.py:13
  127.8 0.0 collective-permute-start.4
  127.8 0.0 copy-done.4
  127.8 5.8 %convolution_convert_fusion = bf16[4096,1024]{1,0:T(8,128)(2,1)} fusion(bf16[96,4096]{1,0:T(8,128)(2,1)S(1)} %fusion.10, bf16[96,1024]{1,0:T(8,128)(2,1)S(1)} %copy-done.2, bf16[96,1024]{1,0:T(8,128)(2,1)S(1)} %copy-done.4, bf16[96,1024]{1,0:T(8,128)(2,1)S(1)} %copy-done.3), kind=kOutput, calls=%fused_computation.1 | convolution fusion | flops 810582016 | bytes 9764864 | tf_op jit(solution)/shard_map/dot_general | solution.py:34
  133.6 0.0 collective-permute-done.5
  133.6 1.6 collective-permute-done.4
  135.2 2.5 fusion.3
  137.7 5.8 %convert_bitcast_fusion = bf16[1024,4096]{0,1:T(8,128)(2,1)} fusion(bf16[96,4096]{1,0:T(8,128)(2,1)S(1)} %fusion.3, bf16[96,1024]{1,0:T(8,128)(2,1)S(1)} %copy-done), kind=kOutput, calls=%fused_computation | convolution fusion | flops 809500672 | bytes 9371648 | tf_op jit(solution)/shard_map/dot_general | solution.py:34
  143.5 0.0 copy-start.6
  143.5 0.0 all-reduce.10.cloned.1.call-update
  143.5 0.0 all-reduce.8.cloned.1.call-start
  143.6 0.6 copy-done.6
  144.2 0.6 dynamic-slice
  145.4 6.8 %convolution_convert_fusion.3 = bf16[96,1024]{1,0:T(8,128)(2,1)} fusion(bf16[96,4096]{1,0:T(8,128)(2,1)S(1)} %fusion.3, bf16[1024,4096]{1,0:T(8,128)(2,1)} %param.9), kind=kOutput, calls=%fused_computation.20 | convolution fusion | flops 805404672 | bytes 9371648 | tf_op jit(solution)/shard_map/dot_general | solution.py:34
  152.2 0.0 all-reduce.8.cloned.1.call-update
  152.2 1.0 fusion.14
  153.2 10.5 %all-reduce = f32[96]{0:T(128)S(1)} all-reduce(f32[96]{0:T(128)S(1)} %neg.13), channel_id=3, replica_groups=mesh['ctx'=4,'row'=4,'col'=2] {'row'}, use_global_device_ids=true, to_apply=%region_3.5.clone | all-reduce | flops 96 | bytes 768
  163.8 0.6 dynamic-slice.1
  164.4 267.9 %all-reduce.10.cloned.1.call-done = (bf16[1024,4096]{0,1:T(8,128)(2,1)}, bf16[4096,1024]{1,0:T(8,128)(2,1)}) async-done(((bf16[1024,4096]{0,1:T(8,128)(2,1)}, bf16[4096,1024]{1,0:T(8,128)(2,1)}), (bf16[1024,4096]{0,1:T(8,128)(2,1)}, bf16[4096,1024]{1,0:T(8,128)(2,1)})) %all-reduce.10.cloned.1.call-update) | async-done | bytes 16777232 | tf_op jit(solution)/shard_map/psum | solution.py:73
  432.3 12.3 %copy.12 = f32[1024,4096]{1,0:T(8,128)} copy(bf16[1024,4096]{0,1:T(8,128)(2,1)} %get-tuple-element.19) | data formatting | bytes 25165824
  444.6 0.0 copy-start.1
  444.6 11.8 %convert_element_type.77 = f32[4096,1024]{1,0:T(8,128)} convert(bf16[4096,1024]{1,0:T(8,128)(2,1)} %get-tuple-element.20) | non-fusion elementwise | flops 4194304 | bytes 25165824 | tf_op jit(solution)/shard_map/convert_element_type | solution.py:61
  456.4 1.0 all-reduce.8.cloned.1.call-done
  457.3 1.6 copy.17
  459.0 0.0 copy-done.1
  (1 shorter events, 0.0 us)
Async XLA Ops:
  7.2 0.9 copy-start
  7.2 32.8 %reduce-scatter.3.cloned.1.call-start = ((), (), s32[]{:S(2)}) async-start(), calls=%async_computation.2 | async-start | bytes 983040 | tf_op jit(solution)/shard_map/reduce_scatter | solution.py:43
  13.8 72.8 %all-reduce.6.cloned.1.call-start = ((), (), s32[]{:S(2)}) async-start(), calls=%async_computation.3 | async-start | bytes 393216 | tf_op jit(solution)/shard_map/psum | solution.py:30
  41.0 9.4 %collective-permute-start = (bf16[24,4096]{1,0:T(8,128)(2,1)S(1)}, bf16[24,4096]{1,0:T(8,128)(2,1)S(1)}, u32[]{:S(2)}, u32[]{:S(2)}) collective-permute-start(bf16[24,4096]{1,0:T(8,128)(2,1)S(1)} %fusion.21), channel_id=1, source_target_pairs={{0,2},{2,4},{4,6},{6,0},{1,3},{3,5},{5,7},{7,1},{8,10},{10,12},{12... | collective-permute-start | bytes 589832 | tf_op jit(solution)/shard_map/ppermute | solution.py:13
  41.1 10.2 %collective-permute-start.2 = (bf16[24,4096]{1,0:T(8,128)(2,1)S(1)}, bf16[24,4096]{1,0:T(8,128)(2,1)S(1)}, u32[]{:S(2)}, u32[]{:S(2)}) collective-permute-start(bf16[24,4096]{1,0:T(8,128)(2,1)S(1)} %fusion.21), channel_id=1, source_target_pairs={{0,6},{2,0},{4,2},{6,4},{1,7},{3,1},{5,3},{7,5},{8,14},{10,8},{12,... | collective-permute-start | bytes 589832 | tf_op jit(solution)/shard_map/ppermute | solution.py:15
  50.4 7.5 %collective-permute-start.1 = (bf16[24,4096]{1,0:T(8,128)(2,1)S(1)}, bf16[24,4096]{1,0:T(8,128)(2,1)S(1)}, u32[]{:S(2)}, u32[]{:S(2)}) collective-permute-start(bf16[24,4096]{1,0:T(8,128)(2,1)S(1)} %collective-permute-done), channel_id=1, source_target_pairs={{0,2},{2,4},{4,6},{6,0},{1,3},{3,5},{5,7},{7,1},{8,10},{10,12},{12... | collective-permute-start | bytes 589832 | tf_op jit(solution)/shard_map/ppermute | solution.py:13
  60.4 26.2 %copy-start.2 = (bf16[96,1024]{1,0:T(8,128)(2,1)S(1)}, bf16[96,1024]{1,0:T(8,128)(2,1)}, u32[]{:S(2)}) copy-start(bf16[96,1024]{1,0:T(8,128)(2,1)} %param.11) | copy-start | bytes 589828
  60.4 26.2 %copy-start.3 = (bf16[96,1024]{1,0:T(8,128)(2,1)S(1)}, bf16[96,1024]{1,0:T(8,128)(2,1)}, u32[]{:S(2)}) copy-start(bf16[96,1024]{1,0:T(8,128)(2,1)} %param.7) | copy-start | bytes 589828
  66.0 51.2 %copy-start.5 = (bf16[24,4096]{1,0:T(8,128)(2,1)S(1)}, bf16[24,4096]{1,0:T(8,128)(2,1)}, u32[]{:S(2)}) copy-start(bf16[24,4096]{1,0:T(8,128)(2,1)} %reduce-scatter.3.cloned.1.call-done) | copy-start | bytes 589828
  66.0 51.2 %reduce-scatter.5.cloned.1.call-start = ((), (), s32[]{:S(2)}) async-start(), calls=%async_computation.4 | async-start | bytes 983040 | tf_op jit(solution)/shard_map/reduce_scatter | solution.py:63
  86.7 41.1 %copy-start.4 = (bf16[96,1024]{1,0:T(8,128)(2,1)S(1)}, bf16[96,1024]{1,0:T(8,128)(2,1)}, u32[]{:S(2)}) copy-start(bf16[96,1024]{1,0:T(8,128)(2,1)} %all-reduce.6.cloned.1.call-done) | copy-start | bytes 589828
  93.8 338.5 %all-reduce.10.cloned.1.call-start = ((), (), s32[]{:S(2)}) async-start(), calls=%async_computation.6 | async-start | bytes 33554432 | tf_op jit(solution)/shard_map/psum | solution.py:73
  118.4 9.4 %collective-permute-start.3 = (bf16[24,4096]{1,0:T(8,128)(2,1)S(1)}, bf16[24,4096]{1,0:T(8,128)(2,1)S(1)}, u32[]{:S(2)}, u32[]{:S(2)}) collective-permute-start(bf16[24,4096]{1,0:T(8,128)(2,1)S(1)} %fusion.25), channel_id=1, source_target_pairs={{0,2},{2,4},{4,6},{6,0},{1,3},{3,5},{5,7},{7,1},{8,10},{10,12},{12... | collective-permute-start | bytes 589832 | tf_op jit(solution)/shard_map/ppermute | solution.py:13
  118.4 15.2 %collective-permute-start.5 = (bf16[24,4096]{1,0:T(8,128)(2,1)S(1)}, bf16[24,4096]{1,0:T(8,128)(2,1)S(1)}, u32[]{:S(2)}, u32[]{:S(2)}) collective-permute-start(bf16[24,4096]{1,0:T(8,128)(2,1)S(1)} %fusion.25), channel_id=1, source_target_pairs={{0,6},{2,0},{4,2},{6,4},{1,7},{3,1},{5,3},{7,5},{8,14},{10,8},{12,... | collective-permute-start | bytes 589832 | tf_op jit(solution)/shard_map/ppermute | solution.py:15
  127.8 7.5 %collective-permute-start.4 = (bf16[24,4096]{1,0:T(8,128)(2,1)S(1)}, bf16[24,4096]{1,0:T(8,128)(2,1)S(1)}, u32[]{:S(2)}, u32[]{:S(2)}) collective-permute-start(bf16[24,4096]{1,0:T(8,128)(2,1)S(1)} %collective-permute-done.3), channel_id=1, source_target_pairs={{0,2},{2,4},{4,6},{6,0},{1,3},{3,5},{5,7},{7,1},{8,10},{10,12},{12... | collective-permute-start | bytes 589832 | tf_op jit(solution)/shard_map/ppermute | solution.py:13
  143.5 0.7 copy-start.6
  143.5 313.8 %all-reduce.8.cloned.1.call-start = ((), (), s32[]{:S(2)}) async-start(), calls=%async_computation.5 | async-start | bytes 393216 | tf_op jit(solution)/shard_map/psum | solution.py:30
  444.6 14.3 %copy-start.1 = (bf16[96,1024]{1,0:T(8,128)(2,1)S(1)}, bf16[96,1024]{1,0:T(8,128)(2,1)}, u32[]{:S(2)}) copy-start(bf16[96,1024]{1,0:T(8,128)(2,1)} %param.8) | copy-start | bytes 589828
Sparse Core Ops, SparseCore 0:
  14.0 25.9 reduce-scatter.2
  66.2 20.4 all-reduce.5
  93.9 23.2 reduce-scatter.4
  143.7 288.5 all-reduce.9
  435.0 22.3 all-reduce.7
